TPU v7x, 32 devices: a whole 2x2x4 slice. The times are simulated.
32 devices in a mesh: groups: 2 (over x), lon: 16 (over z, y, core).
Axes of the slice: x: 2, y: 2, z: 4, core: 2. Of those that a mesh axis runs over, the one named last changes fastest.
Arguments:
- column_state: float32 [2, 32, 2048, 2, 128], P('groups', None, 'lon'), parts along dimension 0, may hold values from -6 to 6
- daylit: int32 [2, 32, 2048], P('groups', None, 'lon'), parts along dimension 0, may hold values from 0 to 1, as said below
- courant_lon: float32 [2, 32, 2048], P('groups', None, 'lon'), parts along dimension 0, may hold values from -0.4 to 0.4
- courant_lat: float32 [2, 32, 2048], P('groups', None, 'lon'), parts along dimension 0, may hold values from -0.4 to 0.4
- w_in: bfloat16 [256, 512], replicated, may hold values from -0.5 to 0.5
- w_mid_a: bfloat16 [512, 512], replicated, may hold values from -0.375 to 0.375
- w_mid_b: bfloat16 [512, 512], replicated, may hold values from -0.375 to 0.375
- w_out: bfloat16 [512, 128], replicated, may hold values from -0.375 to 0.375
Outputs:
- new_state: float32 [2, 32, 2048, 2, 128], P('groups', None, 'lon'), parts along dimension 0
There are 2 independent parts, one for each index of `groups`. A program takes and returns all parts, laid end to end along the dimension named above; an argument that names none is the same for every part. Nothing has to cross between parts.
Inputs may be any that keep to these rules, and one draw needn't show every extreme that they name: In every member and latitude row the daylit columns form one cyclic run of 1024 longitudes, so of the columns at longitudes g and g + 1024 exactly one is daylit.
All inputs are finite; a program needn't handle non-finite values.
Results may differ from a plain program's by a relative error of at most 0.005.
Values may be sent and summed in bfloat16 or wider, within the bound.
A program may use at most 64 MiB of HBM per device.

v0:
```python
import jax
import jax.numpy as jnp
from jax import lax
from jax.sharding import PartitionSpec as P


def padded_2(block, sides, width):
    for axis, dim in sides:
        count = lax.axis_size(axis)
        forward = [(i, i + 1) for i in range(count - 1)]
        forward.append((count - 1, 0))
        backward = [(target, source) for source, target in forward]
        low = lax.ppermute(
            lax.slice_in_dim(block, block.shape[dim] - width, None, axis=dim), axis, forward
        )
        high = lax.ppermute(lax.slice_in_dim(block, 0, width, axis=dim), axis, backward)
        block = jnp.concatenate([low, block, high], axis=dim)
    return block


def shifted(value, axis, steps):
    count = lax.axis_size(axis)
    pairs = [(source, (source + steps) % count) for source in range(count)]
    return lax.ppermute(value, axis, pairs)


def radiate(rows, w_in, w_mid_a, w_mid_b, w_out):
    hidden = jax.nn.silu(jnp.dot(rows, w_in, preferred_element_type=jnp.float32)).astype(
        jnp.bfloat16
    )
    hidden = jax.nn.silu(jnp.dot(hidden, w_mid_a, preferred_element_type=jnp.float32)).astype(
        jnp.bfloat16
    )
    hidden = jax.nn.silu(jnp.dot(hidden, w_mid_b, preferred_element_type=jnp.float32)).astype(
        jnp.bfloat16
    )
    return jnp.dot(hidden, w_out, preferred_element_type=jnp.float32).astype(jnp.bfloat16)


def member_step(column_state, daylit, courant_lon, courant_lat, w_in, w_mid_a, w_mid_b, w_out):
    lat_rows, lon_cols, fields, levels = column_state.shape
    features = fields * levels
    padded = padded_2(column_state.astype(jnp.bfloat16), (("lon", 1),), 1).astype(
        column_state.dtype
    )
    east_cells = padded[:, 2:]
    west_cells = padded[:, :-2]
    lat_padded = jnp.pad(column_state, ((1, 1), (0, 0), (0, 0), (0, 0)))
    north_cells = lat_padded[2:]
    south_cells = lat_padded[:-2]
    push_lon = courant_lon[:, :, None, None]
    push_lat = courant_lat[:, :, None, None]
    tendency = (
        -push_lon * (east_cells - west_cells) * 0.5
        - push_lat * (north_cells - south_cells) * 0.5
        + 0.1 * (east_cells + west_cells + north_cells + south_cells - 4.0 * column_state)
    )
    inputs = column_state.astype(jnp.bfloat16).reshape(lat_rows, lon_cols, features)
    half_rows = lat_rows // 2
    lon_count = lax.axis_size("lon")
    upper_side = lax.axis_index("lon") >= lon_count // 2
    keep_start = jnp.where(upper_side, half_rows, 0).astype(jnp.int32)
    give_start = half_rows - keep_start
    given_inputs = lax.dynamic_slice_in_dim(inputs, give_start, half_rows, 0)
    arrived = shifted(given_inputs, "lon", lon_count // 2)
    own_inputs = lax.dynamic_slice_in_dim(inputs, keep_start, half_rows, 0)
    own_lit = lax.dynamic_slice_in_dim(daylit, keep_start, half_rows, 0)[:, :, None] == 1
    chosen = jnp.where(own_lit, own_inputs, arrived)
    column_rates = radiate(
        chosen.reshape(half_rows * lon_cols, features), w_in, w_mid_a, w_mid_b, w_out
    )
    column_rates = column_rates.reshape(half_rows, lon_cols, levels)
    nothing = jnp.zeros_like(column_rates)
    kept_rates = jnp.where(own_lit, column_rates, nothing)
    sent_rates = jnp.where(own_lit, nothing, column_rates)
    returned = shifted(sent_rates, "lon", lon_count // 2)
    heat_rates = jnp.where(
        upper_side,
        jnp.concatenate([returned, kept_rates], axis=0),
        jnp.concatenate([kept_rates, returned], axis=0),
    )
    heat_field = heat_rates.astype(jnp.float32)
    heating = jnp.stack([heat_field, jnp.zeros_like(heat_field)], axis=2)
    return column_state + tendency + heating


def shards(column_state, daylit, courant_lon, courant_lat, w_in, w_mid_a, w_mid_b, w_out):
    results = [
        member_step(
            column_state[0],
            daylit[0],
            courant_lon[0],
            courant_lat[0],
            w_in,
            w_mid_a,
            w_mid_b,
            w_out,
        )
    ]
    return jnp.stack(results, axis=0)


def solution(mesh):
    placed = (
        P("groups", None, "lon", None, None),
        P("groups", None, "lon"),
        P("groups", None, "lon"),
        P("groups", None, "lon"),
        P(),
        P(),
        P(),
        P(),
    )
    return jax.shard_map(
        shards,
        mesh=mesh,
        in_specs=placed,
        out_specs=P("groups", None, "lon", None, None),
        check_vma=False,
    )
```

profile of v0, /device:TPU:0, one launch (start us, length us, event | category | flops | bytes accessed | tf_op | source)
XLA Modules:
  0.0 105.5 jit_solution(4333020150805757973)
XLA Ops:
  0.0 0.0 copy-start
  0.0 5.3 %convert_element_type.37 = bf16[1,32,128,2,128]{4,3,2,1,0:T(2,128)(2,1)} convert(f32[1,32,128,2,128]{4,3,2,1,0:T(2,128)} %param.8) | non-fusion elementwise | flops 1048576 | bytes 6291456 | tf_op jit(solution)/shard_map/convert_element_type | solution.py:43
  5.3 3.2 %convert_element_type.38 = bf16[32,128,256]{2,1,0:T(8,128)(2,1)S(1)} reshape(bf16[1,32,128,2,128]{4,3,2,1,0:T(2,128)(2,1)} %convert_element_type.37) | data formatting | bytes 4194304 | tf_op jit(solution)/shard_map/convert_element_type | solution.py:43
  8.5 0.0 copy-start.1
  8.5 0.0 copy-start.5
  8.5 0.1 constant_dynamic-slice_fusion
  8.6 1.2 %copy-done.1 = bf16[32,128,256]{2,1,0:T(8,128)(2,1)} copy-done((bf16[32,128,256]{2,1,0:T(8,128)(2,1)}, bf16[32,128,256]{2,1,0:T(8,128)(2,1)S(1)}, u32[]{:S(2)}) %copy-start.1) | copy-done | bytes 2097176
  9.8 4.0 %collective-permute-start.2 = (bf16[16,128,256]{2,1,0:T(8,128)(2,1)S(1)}, bf16[16,128,256]{2,1,0:T(8,128)(2,1)S(1)}, u32[]{:S(2)}, u32[]{:S(2)}) collective-permute-start(bf16[16,128,256]{2,1,0:T(8,128)(2,1)S(1)} %constant_dynamic-slice_fusion), channel_id=1, source_target_pairs={{0,8},{1,9},{2,10},{3,11},{4,12},{5,13},{6,14},{7,15},{8,0},{9,1},... | collective-permute-start | bytes 3145736 | tf_op jit(solution)/shard_map/ppermute | solution.py:24
  13.8 2.9 %copy.15 = bf16[1,32,128,2,128]{4,2,1,3,0:T(8,128)(2,1)S(1)} copy(f32[1,32,128,2,128]{4,3,2,1,0:T(2,128)} %param.8) | data formatting | bytes 6291456 | tf_op args[0]
  16.8 0.0 copy-done.5
  16.8 42.6 %collective-permute-done.2 = bf16[16,128,256]{2,1,0:T(8,128)(2,1)S(1)} collective-permute-done((bf16[16,128,256]{2,1,0:T(8,128)(2,1)S(1)}, bf16[16,128,256]{2,1,0:T(8,128)(2,1)S(1)}, u32[]{:S(2)}, u32[]{:S(2)}) %collective-permute-start.2) | collective-permute-done | bytes 1048608 | tf_op jit(solution)/shard_map/ppermute | solution.py:24
  59.5 0.0 copy-done.2
  59.5 1.2 %dynamic-slice_select_fusion = bf16[16,128,256]{2,1,0:T(8,128)(2,1)} fusion(bf16[16,128,256]{2,1,0:T(8,128)(2,1)S(1)} %collective-permute-done.2, bf16[32,128,256]{2,1,0:T(8,128)(2,1)S(1)} %copy-done.2, s32[]{:T(128)S(6)} %select_n.45, pred[16,128]{1,0:T(8,128)(4,1)S(1)} %fusion.2), kind=kLoop, calls=%fused_computation.12 | loop fusion | flops 524288 | bytes 3147780 | tf_op jit(solution)/shard_map/jit(_where)/select_n | solution.py:68
  60.7 0.0 copy-done
  60.7 0.0 copy-done.6
  60.7 5.5 %fusion.1 = f32[2048,512]{1,0:T(8,128)} fusion(bf16[512,512]{1,0:T(8,128)(2,1)S(1)} %copy-done, bf16[2048,256]{1,0:T(8,128)(2,1)} %bitcast.26, bf16[256,512]{1,0:T(8,128)(2,1)S(1)} %copy-done.6), kind=kOutput, calls=%fused_computation.10 | convolution fusion | flops 1615855616 | bytes 6029312 | tf_op jit(solution)/shard_map/dot_general | solution.py:31
  66.2 0.0 copy-done.7
  66.2 5.2 %convolution_convert_fusion = bf16[2048,128]{1,0:T(8,128)(2,1)S(1)} fusion(bf16[512,128]{1,0:T(8,128)(2,1)S(1)} %copy-done.7, bf16[512,512]{1,0:T(8,128)(2,1)} %param.14, f32[2048,512]{1,0:T(8,128)} %fusion.1), kind=kOutput, calls=%fused_computation.7 | convolution fusion | flops 1352925184 | bytes 5373952 | tf_op jit(solution)/shard_map/dot_general | solution.py:37
  71.4 0.4 broadcast_select_fusion
  71.9 0.1 collective-permute-start.3
  71.9 0.1 fusion.7
  72.0 0.1 collective-permute-start
  72.1 4.4 %collective-permute-start.1 = (bf16[32,1,2,128]{3,1,0,2:T(2,128)(2,1)S(1)}, bf16[32,1,2,128]{3,1,0,2:T(2,128)(2,1)S(1)}, u32[]{:S(2)}, u32[]{:S(2)}) collective-permute-start(bf16[32,1,2,128]{3,1,0,2:T(2,128)(2,1)S(1)} %get-tuple-element.6), channel_id=1, source_target_pairs={{1,0},{2,1},{3,2},{4,3},{5,4},{6,5},{7,6},{8,7},{9,8},{10,9},{11,1... | collective-permute-start | bytes 49160 | tf_op jit(solution)/shard_map/ppermute | solution.py:16
  76.5 2.7 %copy.14 = f32[1,32,128,2,128]{4,2,1,3,0:T(8,128)S(1)} copy(f32[1,32,128,2,128]{4,3,2,1,0:T(2,128)} %param.8) | data formatting | bytes 8388608 | tf_op args[0]
  79.3 0.0 copy-start.4
  79.3 9.4 %collective-permute-done = bf16[32,1,2,128]{3,1,0,2:T(2,128)(2,1)S(1)} collective-permute-done((bf16[32,1,2,128]{3,1,0,2:T(2,128)(2,1)S(1)}, bf16[32,1,2,128]{3,1,0,2:T(2,128)(2,1)S(1)}, u32[]{:S(2)}, u32[]{:S(2)}) %collective-permute-start) | collective-permute-done | bytes 16416 | tf_op jit(solution)/shard_map/ppermute | solution.py:13
  88.7 0.0 collective-permute-done.1
  88.7 0.8 maximum_convert_fusion
  89.6 7.6 %collective-permute-done.3 = bf16[16,128,128]{2,1,0:T(8,128)(2,1)S(1)} collective-permute-done((bf16[16,128,128]{2,1,0:T(8,128)(2,1)S(1)}, bf16[16,128,128]{2,1,0:T(8,128)(2,1)S(1)}, u32[]{:S(2)}, u32[]{:S(2)}) %collective-permute-start.3) | collective-permute-done | bytes 524320 | tf_op jit(solution)/shard_map/ppermute | solution.py:24
  97.2 0.2 maximum_select_fusion
  97.3 2.8 %add_bitcast_fusion = f32[1,32,128,2,128]{4,2,1,3,0:T(8,128)S(1)} fusion(f32[32,128,2,128]{3,1,0,2:T(8,128)S(1)} %bitcast.23, f32[32,130,2,128]{3,1,0,2:T(8,128)S(1)} %maximum_convert_fusion, bf16[32,128,1,128]{3,1,0,2:T(8,128)(2,1)S(1)} %maximum_select_fusion, f32[32,128]{1,0:T(8,128)S(1)} %bitcast.29, f32[32,128]{1,0:T(8,128)S(1)} %negate_bitcast_fusion), kind=kLoop, calls=%fused_computation.3 | loop fusion | flops 17825792 | bytes 17858560 | tf_op jit(solution)/shard_map/stack | solution.py:100
  100.2 5.3 %copy.10 = f32[1,32,128,2,128]{4,3,2,1,0:T(2,128)} copy(f32[1,32,128,2,128]{4,2,1,3,0:T(8,128)S(1)} %add_bitcast_fusion) | data formatting | bytes 8388608 | tf_op jit(solution)/shard_map/stack | solution.py:100
  (8 shorter events, 0.0 us)
Async XLA Ops:
  0.0 60.7 %copy-start = (bf16[512,512]{1,0:T(8,128)(2,1)S(1)}, bf16[512,512]{1,0:T(8,128)(2,1)}, u32[]{:S(2)}) copy-start(bf16[512,512]{1,0:T(8,128)(2,1)} %param.13) | copy-start | bytes 1572868
  8.5 1.3 %copy-start.1 = (bf16[32,128,256]{2,1,0:T(8,128)(2,1)}, bf16[32,128,256]{2,1,0:T(8,128)(2,1)S(1)}, u32[]{:S(2)}) copy-start(bf16[32,128,256]{2,1,0:T(8,128)(2,1)S(1)} %convert_element_type.38) | copy-start | bytes 6291460
  8.5 8.3 %copy-start.5 = (s32[1,32,128]{2,1,0:T(8,128)S(1)}, s32[1,32,128]{2,1,0:T(8,128)}, u32[]{:S(2)}) copy-start(s32[1,32,128]{2,1,0:T(8,128)} %param.9) | copy-start | bytes 49156
  9.8 50.9 %copy-start.6 = (bf16[256,512]{1,0:T(8,128)(2,1)S(1)}, bf16[256,512]{1,0:T(8,128)(2,1)}, u32[]{:S(2)}) copy-start(bf16[256,512]{1,0:T(8,128)(2,1)} %param.12) | copy-start | bytes 786436
  9.8 49.7 %collective-permute-start.2 = (bf16[16,128,256]{2,1,0:T(8,128)(2,1)S(1)}, bf16[16,128,256]{2,1,0:T(8,128)(2,1)S(1)}, u32[]{:S(2)}, u32[]{:S(2)}) collective-permute-start(bf16[16,128,256]{2,1,0:T(8,128)(2,1)S(1)} %constant_dynamic-slice_fusion), channel_id=1, source_target_pairs={{0,8},{1,9},{2,10},{3,11},{4,12},{5,13},{6,14},{7,15},{8,0},{9,1},... | collective-permute-start | bytes 3145736 | tf_op jit(solution)/shard_map/ppermute | solution.py:24
  13.8 45.6 %copy-start.2 = (bf16[32,128,256]{2,1,0:T(8,128)(2,1)S(1)}, bf16[32,128,256]{2,1,0:T(8,128)(2,1)}, u32[]{:S(2)}) copy-start(bf16[32,128,256]{2,1,0:T(8,128)(2,1)} %copy-done.1) | copy-start | bytes 6291460
  60.7 5.5 %copy-start.7 = (bf16[512,128]{1,0:T(8,128)(2,1)S(1)}, bf16[512,128]{1,0:T(8,128)(2,1)}, u32[]{:S(2)}) copy-start(bf16[512,128]{1,0:T(8,128)(2,1)} %param.15) | copy-start | bytes 393220
  66.2 10.3 %copy-start.3 = (f32[1,32,128]{2,1,0:T(8,128)S(1)}, f32[1,32,128]{2,1,0:T(8,128)}, u32[]{:S(2)}) copy-start(f32[1,32,128]{2,1,0:T(8,128)} %param.10) | copy-start | bytes 49156
  71.9 25.3 %collective-permute-start.3 = (bf16[16,128,128]{2,1,0:T(8,128)(2,1)S(1)}, bf16[16,128,128]{2,1,0:T(8,128)(2,1)S(1)}, u32[]{:S(2)}, u32[]{:S(2)}) collective-permute-start(bf16[16,128,128]{2,1,0:T(8,128)(2,1)S(1)} %get-tuple-element.7), channel_id=1, source_target_pairs={{0,8},{1,9},{2,10},{3,11},{4,12},{5,13},{6,14},{7,15},{8,0},{9,1},... | collective-permute-start | bytes 1572872 | tf_op jit(solution)/shard_map/ppermute | solution.py:24
  72.0 16.7 %collective-permute-start = (bf16[32,1,2,128]{3,1,0,2:T(2,128)(2,1)S(1)}, bf16[32,1,2,128]{3,1,0,2:T(2,128)(2,1)S(1)}, u32[]{:S(2)}, u32[]{:S(2)}) collective-permute-start(bf16[32,1,2,128]{3,1,0,2:T(2,128)(2,1)S(1)} %get-tuple-element.5), channel_id=1, source_target_pairs={{0,1},{1,2},{2,3},{3,4},{4,5},{5,6},{6,7},{7,8},{8,9},{9,10},{10,1... | collective-permute-start | bytes 49160 | tf_op jit(solution)/shard_map/ppermute | solution.py:13
  72.1 16.6 %collective-permute-start.1 = (bf16[32,1,2,128]{3,1,0,2:T(2,128)(2,1)S(1)}, bf16[32,1,2,128]{3,1,0,2:T(2,128)(2,1)S(1)}, u32[]{:S(2)}, u32[]{:S(2)}) collective-permute-start(bf16[32,1,2,128]{3,1,0,2:T(2,128)(2,1)S(1)} %get-tuple-element.6), channel_id=1, source_target_pairs={{1,0},{2,1},{3,2},{4,3},{5,4},{6,5},{7,6},{8,7},{9,8},{10,9},{11,1... | collective-permute-start | bytes 49160 | tf_op jit(solution)/shard_map/ppermute | solution.py:16
  79.3 18.1 %copy-start.4 = (f32[1,32,128]{2,1,0:T(8,128)S(1)}, f32[1,32,128]{2,1,0:T(8,128)}, u32[]{:S(2)}) copy-start(f32[1,32,128]{2,1,0:T(8,128)} %param.11) | copy-start | bytes 49156
where the time goes:
time: 106 us; the launch traced here: 105 us
  waiting for transfers between devices  59.7 us (56%)
  local copies, waits for them, and re-layouts  15.5 us (15%)
  other arithmetic  10.8 us (10%)
  matrix products  10.7 us (10%)
  starting transfers between devices  8.6 us (8%)
    ppermute x2, waiting for transfers between devices, shifted(): return lax.ppermute(value, axis, pairs)  50.2 us
    ppermute x1, waiting for transfers between devices, padded_2(): lax.ppermute(lax.slice_in_dim(block, block.shape[dim] - width, None, axis...  9.45 us
    unnamed x18, local copies, waits for them, and re-layouts  6.92 us
    dot_general x1, matrix products, radiate(): jnp.dot(hidden, w_mid_a, preferred_element_type=jnp.float32)  5.49 us
    convert_element_type x1, other arithmetic, member_step(): column_state.astype(jnp.bfloat16)  5.32 us
    another operation x1, local copies, waits for them, and re-layouts, shards(): return jnp.stack(results, axis=0)  5.3 us
    dot_general x1, matrix products, radiate(): jnp.dot(hidden, w_out, preferred_element_type=jnp.float32)  5.21 us
    ppermute x1, starting transfers between devices, padded_2(): lax.ppermute(lax.slice_in_dim(block, 0, width, axis=dim), axis, backward)  4.43 us
  transfers between devices with their start and end apart: 4, of which 3 were waited for; matrix products, arithmetic and copies ran while one was open for 6% of the time, Pallas kernels for 0%

commit v1 on v0

v1 whole, which is shorter than its diff:
```python
import functools

import jax
import jax.numpy as jnp
from jax import lax
from jax.experimental import pallas as pl
from jax.experimental.pallas import tpu as pltpu
from jax.sharding import PartitionSpec as P

PAD = 8


def silu_half(half):
    return half + half * jnp.tanh(half)


def column_kernel(chunk, x_hbm, coef_hbm, low_hbm, high_hbm, w_in_hbm, w_a_hbm, w_b_hbm, w_out_hbm,
                  out_hbm, xs, outs, coef, low, high, turned, w_in, w_a, w_b, w_out,
                  x_sems, w_sems, out_sems):
    lat, width, lev = x_hbm.shape
    cols = width // 2
    steps = lat // chunk

    def x_copy(i):
        return pltpu.make_async_copy(
            x_hbm.at[pl.ds(i * chunk, chunk)],
            xs.at[pl.ds(1 + i * chunk, chunk), pl.ds(PAD, width)],
            x_sems.at[i],
        )

    def out_copy(i):
        return pltpu.make_async_copy(
            outs.at[pl.ds(i * chunk, chunk)], out_hbm.at[pl.ds(i * chunk, chunk)], out_sems.at[i]
        )

    smalls = [
        pltpu.make_async_copy(source, target, w_sems.at[k])
        for k, (source, target) in enumerate([
            (w_in_hbm, w_in), (w_a_hbm, w_a), (w_b_hbm, w_b), (w_out_hbm, w_out),
            (coef_hbm, coef), (low_hbm, low), (high_hbm, high),
        ])
    ]
    x_copy(0).start()
    for copy in smalls:
        copy.start()

    @pl.loop(1, steps)
    def _(i):
        x_copy(i).start()

    blank = jnp.zeros((width, lev), jnp.float32)
    xs[0, pl.ds(PAD, width)] = blank
    xs[lat + 1, pl.ds(PAD, width)] = blank
    for copy in smalls:
        copy.wait()
    for w in (w_in, w_a, w_b):
        w[...] = w[...] * jnp.bfloat16(0.5)
    turned[...] = coef[...].T
    xs[pl.ds(1, lat), pl.ds(PAD - 2, 2)] = low[...].astype(jnp.float32)
    xs[pl.ds(1, lat), pl.ds(PAD + width, 2)] = high[...].astype(jnp.float32)
    x_copy(0).wait()

    def picked(r):
        at = jnp.full((cols, 128), r, jnp.int32)
        return jnp.take_along_axis(turned[...], at, axis=1, mode="promise_in_bounds")

    @pl.loop(0, steps)
    def _(i):
        @pl.when(i < steps - 1)
        def _():
            x_copy(i + 1).wait()

        first = i * chunk
        rows = []
        for q in range(chunk):
            rows.append(jnp.concatenate([
                xs[1 + first + q, pl.ds(PAD + f, cols, stride=2), :].astype(jnp.bfloat16)
                for f in range(2)
            ], axis=1))
        hidden = jnp.concatenate(rows, axis=0)
        for w in (w_in, w_a, w_b):
            hidden = silu_half(
                jnp.dot(hidden, w[...], preferred_element_type=jnp.float32)
            ).astype(jnp.bfloat16)
        rates = jnp.dot(hidden, w_out[...], preferred_element_type=jnp.float32)
        for q in range(chunk):
            r = first + q
            push_lon = picked(r)
            push_lat = picked(lat + r)
            lit = picked(2 * lat + r)
            heat = jnp.where(lit > 0.5, rates[q * cols:(q + 1) * cols], 0.0)
            for f in range(2):
                mid = xs[1 + r, pl.ds(PAD + f, cols, stride=2), :]
                east = xs[1 + r, pl.ds(PAD + 2 + f, cols, stride=2), :]
                west = xs[1 + r, pl.ds(PAD - 2 + f, cols, stride=2), :]
                north = xs[2 + r, pl.ds(PAD + f, cols, stride=2), :]
                south = xs[r, pl.ds(PAD + f, cols, stride=2), :]
                new = (0.6 * mid + 0.1 * ((east + west) + (north + south))
                       - push_lon * (east - west) - push_lat * (north - south))
                if f == 0:
                    new = new + heat
                outs[r, pl.ds(f, cols, stride=2), :] = new
        out_copy(i).start()

    @pl.loop(0, steps)
    def _(i):
        out_copy(i).wait()


def column_step(x, coef, low, high, w_in, w_a, w_b, w_out, chunk):
    lat, width, lev = x.shape
    steps = lat // chunk
    anywhere = pl.BlockSpec(memory_space=pl.ANY)
    return pl.pallas_call(
        functools.partial(column_kernel, chunk),
        out_shape=jax.ShapeDtypeStruct(x.shape, jnp.float32),
        in_specs=[anywhere] * 8,
        out_specs=anywhere,
        scratch_shapes=[
            pltpu.VMEM((lat + 2, width + 2 * PAD, lev), jnp.float32),
            pltpu.VMEM(x.shape, jnp.float32),
            pltpu.VMEM(coef.shape, jnp.float32),
            pltpu.VMEM(low.shape, low.dtype),
            pltpu.VMEM(high.shape, high.dtype),
            pltpu.VMEM(coef.shape[::-1], jnp.float32),
            pltpu.VMEM(w_in.shape, w_in.dtype),
            pltpu.VMEM(w_a.shape, w_a.dtype),
            pltpu.VMEM(w_b.shape, w_b.dtype),
            pltpu.VMEM(w_out.shape, w_out.dtype),
            pltpu.SemaphoreType.DMA((steps,)),
            pltpu.SemaphoreType.DMA((7,)),
            pltpu.SemaphoreType.DMA((steps,)),
        ],
        compiler_params=pltpu.CompilerParams(vmem_limit_bytes=48 * 1024 * 1024),
        cost_estimate=pl.CostEstimate(
            flops=2 * lat * width // 2 * 720896, bytes_accessed=10 * 1024 * 1024,
            transcendentals=lat * width // 2 * 1536,
        ),
        name="column_step",
    )(x, coef, low, high, w_in, w_a, w_b, w_out)


def shards(column_state, daylit, courant_lon, courant_lat, w_in, w_mid_a, w_mid_b, w_out):
    _, lat, cols, fields, lev = column_state.shape
    count = lax.axis_size("lon")
    state = column_state[0]
    up = [(i, (i + 1) % count) for i in range(count)]
    down = [(b, a) for a, b in up]
    low = lax.ppermute(state[:, cols - 1].astype(jnp.bfloat16), "lon", up)
    high = lax.ppermute(state[:, 0].astype(jnp.bfloat16), "lon", down)
    coef = jnp.concatenate([
        0.5 * courant_lon[0], 0.5 * courant_lat[0], daylit[0].astype(jnp.float32),
        jnp.zeros((128 - 3 * lat, cols), jnp.float32),
    ], axis=0)
    out = column_step(
        state.reshape(lat, cols * fields, lev), coef, low, high, w_in, w_mid_a, w_mid_b, w_out, 4
    )
    return out.reshape(column_state.shape)


def solution(mesh):
    placed = (
        P("groups", None, "lon", None, None),
        P("groups", None, "lon"),
        P("groups", None, "lon"),
        P("groups", None, "lon"),
        P(),
        P(),
        P(),
        P(),
    )
    return jax.shard_map(
        shards,
        mesh=mesh,
        in_specs=placed,
        out_specs=P("groups", None, "lon", None, None),
        check_vma=False,
    )
```

time: 106 us -> 27.8 us (0.26)
  waiting for transfers between devices: 59.7 us -> 5.66 us
  Pallas kernels: 0 us -> 11.5 us
  other arithmetic: 10.8 us -> 0.09 us
  matrix products: 10.7 us -> 0 us
  local copies, waits for them, and re-layouts: 15.5 us -> 4.86 us
  starting transfers between devices: 8.6 us -> 5.51 us
    ppermute x4 -> x2, waiting for transfers between devices: 59.7 us -> 5.66 us  [the longest x1 4.42 us: shards(): low = lax.ppermute(state[:, cols - 1].astype(jnp.bfloat16), 'lon', up)]
    pallas_call x0 -> x1, Pallas kernels: none -> 11.5 us  [column_step(): pl.pallas_call(functools.partial(column_kernel, chunk), out_shape=jax.Sha...]
    dot_general x2 -> x0, matrix products: 10.7 us -> none  [the longest x1 5.49 us: radiate(): jnp.dot(hidden, w_mid_a, preferred_element_type=jnp.float32)]
    convert_element_type x2 -> x1, other arithmetic: 6.17 us -> 0.01 us  [shards(): daylit[0].astype(jnp.float32)]
    another operation x1 -> x0, local copies, waits for them, and re-layouts: 5.3 us -> none  [shards(): return jnp.stack(results, axis=0)]
    convert_element_type x1, local copies, waits for them, and re-layouts: 3.15 us -> 0.03 us  [shards(): high = lax.ppermute(state[:, 0].astype(jnp.bfloat16), 'lon', down)]
    ppermute x4 -> x2, starting transfers between devices: 8.6 us -> 5.51 us  [the longest x1 5.51 us: shards(): high = lax.ppermute(state[:, 0].astype(jnp.bfloat16), 'lon', down)]
    another operation x1 -> x0, other arithmetic: 2.84 us -> none  [shards(): return jnp.stack(results, axis=0)]
  transfers between devices with their start and end apart: 4 -> 2, of which waited for: 3 -> 2; matrix products, arithmetic and copies ran while one was open for 6% -> 1% of each run, Pallas kernels for 0% -> 0%
where the time goes in v1:
time: 27.8 us; the launch traced here: 27.7 us
  Pallas kernels  11.5 us (41%)
  waiting for transfers between devices  5.66 us (20%)
  starting transfers between devices  5.51 us (20%)
  local copies, waits for them, and re-layouts  4.86 us (17%)
    pallas_call x1, Pallas kernels, column_step(): pl.pallas_call(functools.partial(column_kernel, chunk), out_shape=jax.Sha...  11.5 us
    ppermute x1, starting transfers between devices, shards(): high = lax.ppermute(state[:, 0].astype(jnp.bfloat16), 'lon', down)  5.51 us
    unnamed x17, local copies, waits for them, and re-layouts  4.75 us
    ppermute x1, waiting for transfers between devices, shards(): low = lax.ppermute(state[:, cols - 1].astype(jnp.bfloat16), 'lon', up)  4.42 us
    ppermute x1, waiting for transfers between devices, shards(): high = lax.ppermute(state[:, 0].astype(jnp.bfloat16), 'lon', down)  1.25 us
  transfers between devices with their start and end apart: 2, of which 2 were waited for; matrix products, arithmetic and copies ran while one was open for 1% of the time, Pallas kernels for 0%

profile of v1, /device:TPU:0, one launch (start us, length us, event | category | flops | bytes accessed | tf_op | source)
XLA Modules:
  0.0 27.7 jit_solution(7930902397493926774)
XLA Ops:
  0.0 0.0 copy-start
  0.0 0.0 copy-start.5
  0.0 0.0 copy-start.6
  0.0 0.0 copy-start.7
  0.0 0.0 copy-start.4
  0.0 0.0 copy-start.2
  0.0 0.0 copy-start.1
  0.0 0.0 copy-start.3
  0.0 4.7 %copy.13 = bf16[1,32,128,2,128]{4,3,1,2,0:T(2,128)(2,1)S(1)} copy(f32[1,32,128,2,128]{4,3,2,1,0:T(2,128)} %param.8) | data formatting | bytes 6291456 | tf_op args[0]
  4.8 5.5 %collective-permute-start.1 = (bf16[32,2,128]{2,1,0:T(2,128)(2,1)S(1)}, bf16[32,2,128]{2,1,0:T(2,128)(2,1)S(1)}, u32[]{:S(2)}, u32[]{:S(2)}) collective-permute-start(bf16[32,2,128]{2,1,0:T(2,128)(2,1)S(1)} %get-tuple-element.5), channel_id=1, source_target_pairs={{1,0},{2,1},{3,2},{4,3},{5,4},{6,5},{7,6},{8,7},{9,8},{10,9},{11,1... | collective-permute-start | bytes 49160 | tf_op jit(solution)/shard_map/ppermute | solution.py:150
  10.3 0.0 collective-permute-start
  10.3 0.0 copy-done.5
  10.3 0.1 pad.3.clone
  10.4 0.0 copy-done.6
  10.4 0.0 copy-done.7
  10.4 0.1 maximum_maximum_fusion.coef_hbm
  10.5 1.2 %collective-permute-done.1.high_hbm = bf16[32,2,128]{2,1,0:T(2,128)(2,1)S(1)} collective-permute-done((bf16[32,2,128]{2,1,0:T(2,128)(2,1)S(1)}, bf16[32,2,128]{2,1,0:T(2,128)(2,1)S(1)}, u32[]{:S(2)}, u32[]{:S(2)}) %collective-permute-start.1) | collective-permute-done | bytes 16416 | tf_op jit(solution)/shard_map/ppermute | solution.py:150
  11.8 4.4 %collective-permute-done.low_hbm = bf16[32,2,128]{2,1,0:T(2,128)(2,1)S(1)} collective-permute-done((bf16[32,2,128]{2,1,0:T(2,128)(2,1)S(1)}, bf16[32,2,128]{2,1,0:T(2,128)(2,1)S(1)}, u32[]{:S(2)}, u32[]{:S(2)}) %collective-permute-start) | collective-permute-done | bytes 16416 | tf_op jit(solution)/shard_map/ppermute | solution.py:149
  16.2 0.0 copy-done
  16.2 0.0 copy-done.4
  16.2 0.0 copy-done.2
  16.2 0.0 copy-done.1
  16.2 0.0 copy-done.3
  16.2 11.5 %column_step.1 = f32[32,256,128]{2,1,0:T(8,128)} custom-call(f32[32,256,128]{2,1,0:T(8,128)S(1)} %bitcast.15, f32[128,128]{1,0:T(8,128)S(1)} %maximum_maximum_fusion.coef_hbm, bf16[32,2,128]{2,1,0:T(2,128)(2,1)S(1)} %collective-permute-done.low_hbm, bf16[32,2,128]{2,1,0:T(2,128)(2,1)S(1)} %collective-permute-done.1.high_hbm, bf16[256,512]{1,0:T(8,128)(2,1)S(1)} %copy-done.3, ...), custom_call_target="tpu_custom_call" | custom-call | flops 5905580032 | bytes 10485760 | tf_op jit(solution)/shard_map/column_step/pallas_call | solution.py:114
  (4 shorter events, 0.0 us)
Async XLA Ops:
  0.0 16.2 %copy-start = (f32[1,32,128,2,128]{4,3,2,1,0:T(2,128)S(1)}, f32[1,32,128,2,128]{4,3,2,1,0:T(2,128)}, u32[]{:S(2)}) copy-start(f32[1,32,128,2,128]{4,3,2,1,0:T(2,128)} %param.8) | copy-start | bytes 12582916
  0.0 10.3 %copy-start.5 = (s32[1,32,128]{2,1,0:T(8,128)S(1)}, s32[1,32,128]{2,1,0:T(8,128)}, u32[]{:S(2)}) copy-start(s32[1,32,128]{2,1,0:T(8,128)} %param.9) | copy-start | bytes 49156
  0.0 10.4 %copy-start.6 = (f32[1,32,128]{2,1,0:T(8,128)S(1)}, f32[1,32,128]{2,1,0:T(8,128)}, u32[]{:S(2)}) copy-start(f32[1,32,128]{2,1,0:T(8,128)} %param.11) | copy-start | bytes 49156
  0.0 10.4 %copy-start.7 = (f32[1,32,128]{2,1,0:T(8,128)S(1)}, f32[1,32,128]{2,1,0:T(8,128)}, u32[]{:S(2)}) copy-start(f32[1,32,128]{2,1,0:T(8,128)} %param.10) | copy-start | bytes 49156
  0.0 16.2 %copy-start.4 = (bf16[512,128]{1,0:T(8,128)(2,1)S(1)}, bf16[512,128]{1,0:T(8,128)(2,1)}, u32[]{:S(2)}) copy-start(bf16[512,128]{1,0:T(8,128)(2,1)} %w_out_hbm.1) | copy-start | bytes 393220
  0.0 16.2 %copy-start.2 = (bf16[512,512]{1,0:T(8,128)(2,1)S(1)}, bf16[512,512]{1,0:T(8,128)(2,1)}, u32[]{:S(2)}) copy-start(bf16[512,512]{1,0:T(8,128)(2,1)} %w_b_hbm.1) | copy-start | bytes 1572868
  0.0 16.2 %copy-start.1 = (bf16[512,512]{1,0:T(8,128)(2,1)S(1)}, bf16[512,512]{1,0:T(8,128)(2,1)}, u32[]{:S(2)}) copy-start(bf16[512,512]{1,0:T(8,128)(2,1)} %w_a_hbm.1) | copy-start | bytes 1572868
  0.0 16.2 %copy-start.3 = (bf16[256,512]{1,0:T(8,128)(2,1)S(1)}, bf16[256,512]{1,0:T(8,128)(2,1)}, u32[]{:S(2)}) copy-start(bf16[256,512]{1,0:T(8,128)(2,1)} %w_in_hbm.1) | copy-start | bytes 786436
  4.8 7.0 %collective-permute-start.1 = (bf16[32,2,128]{2,1,0:T(2,128)(2,1)S(1)}, bf16[32,2,128]{2,1,0:T(2,128)(2,1)S(1)}, u32[]{:S(2)}, u32[]{:S(2)}) collective-permute-start(bf16[32,2,128]{2,1,0:T(2,128)(2,1)S(1)} %get-tuple-element.5), channel_id=1, source_target_pairs={{1,0},{2,1},{3,2},{4,3},{5,4},{6,5},{7,6},{8,7},{9,8},{10,9},{11,1... | collective-permute-start | bytes 49160 | tf_op jit(solution)/shard_map/ppermute | solution.py:150
  10.3 5.9 %collective-permute-start = (bf16[32,2,128]{2,1,0:T(2,128)(2,1)S(1)}, bf16[32,2,128]{2,1,0:T(2,128)(2,1)S(1)}, u32[]{:S(2)}, u32[]{:S(2)}) collective-permute-start(bf16[32,2,128]{2,1,0:T(2,128)(2,1)S(1)} %get-tuple-element.6), channel_id=1, source_target_pairs={{0,1},{1,2},{2,3},{3,4},{4,5},{5,6},{6,7},{7,8},{8,9},{9,10},{10,1... | collective-permute-start | bytes 49160 | tf_op jit(solution)/shard_map/ppermute | solution.py:149

commit v2 on v1

v2 whole, which is shorter than its diff:
```python
import functools

import jax
import jax.numpy as jnp
from jax import lax
from jax.experimental import pallas as pl
from jax.experimental.pallas import tpu as pltpu
from jax.sharding import PartitionSpec as P

PAD = 8
EARLY_MIB = 58


def silu_half(half):
    return half + half * jnp.tanh(half)


def halved(*weights):
    for w in weights:
        w[...] = w[...] * jnp.bfloat16(0.5)


def network(hidden, weights, w_out):
    for w in weights:
        hidden = silu_half(
            jnp.dot(hidden, w[...], preferred_element_type=jnp.float32)
        ).astype(jnp.bfloat16)
    return jnp.dot(hidden, w_out[...], preferred_element_type=jnp.float32)


def early_kernel(chunk, early, x_hbm, w_in_hbm, w_a_hbm, w_b_hbm, w_out_hbm,
                 rates_ref, low_ref, high_ref,
                 xs, edges, packed, landed, w_in, w_a, w_b, w_out,
                 x_sems, w_sems, edge_sems, send_sems, recv_sems):
    lat, width, lev = x_hbm.shape
    cols = width // 2
    steps = early // chunk
    count = lax.axis_size("lon")
    me = lax.axis_index("lon")
    right = lax.rem(me + 1, count)
    left = lax.rem(me + count - 1, count)
    barrier = pltpu.get_barrier_semaphore()
    for other in (left, right):
        pl.semaphore_signal(
            barrier, inc=1, device_id={"lon": other}, device_id_type=pl.DeviceIdType.MESH
        )

    def x_copy(i):
        return pltpu.make_async_copy(
            x_hbm.at[pl.ds(i * chunk, chunk)], xs.at[pl.ds(i * chunk, chunk)], x_sems.at[i]
        )

    edge_copies = [
        pltpu.make_async_copy(
            x_hbm.at[:, pl.ds(start, PAD)], edges.at[side], edge_sems.at[side]
        )
        for side, start in enumerate((0, width - PAD))
    ]
    w_copies = [
        pltpu.make_async_copy(source, target, w_sems.at[k])
        for k, (source, target) in enumerate([
            (w_in_hbm, w_in), (w_a_hbm, w_a), (w_b_hbm, w_b), (w_out_hbm, w_out),
        ])
    ]
    w_copies[0].start()
    x_copy(0).start()
    for copy in w_copies[1:]:
        copy.start()
    for copy in edge_copies:
        copy.start()
    for i in range(1, steps):
        x_copy(i).start()

    sends = [
        pltpu.make_async_remote_copy(
            src_ref=packed.at[side], dst_ref=landed.at[side],
            send_sem=send_sems.at[side], recv_sem=recv_sems.at[side],
            device_id={"lon": other}, device_id_type=pl.DeviceIdType.MESH,
        )
        for side, other in enumerate((left, right))
    ]
    for copy in w_copies:
        copy.wait()
    halved(w_in, w_a, w_b)
    for side, copy in enumerate(edge_copies):
        copy.wait()
        for f in range(2):
            inner = f if side == 0 else PAD - 2 + f
            packed[side, pl.ds(f * lat, lat)] = edges[side, :, inner, :]

    @pl.loop(0, steps)
    def _(i):
        @pl.when(i == 1)
        def _():
            pl.semaphore_wait(barrier, 2)
            for send in sends:
                send.start()

        x_copy(i).wait()
        rows = [
            jnp.concatenate([
                xs[i * chunk + q, pl.ds(f, cols, stride=2), :].astype(jnp.bfloat16)
                for f in range(2)
            ], axis=1)
            for q in range(chunk)
        ]
        rates = network(jnp.concatenate(rows, axis=0), (w_in, w_a, w_b), w_out)
        rates_ref[pl.ds(i * chunk, chunk)] = rates.astype(jnp.bfloat16).reshape(chunk, cols, lev)

    for send in sends:
        send.wait()
    high_ref[...] = landed[0]
    low_ref[...] = landed[1]


def early_part(x, w_in, w_a, w_b, w_out, chunk, early):
    lat, width, lev = x.shape
    steps = early // chunk
    anywhere = pl.BlockSpec(memory_space=pl.ANY)
    kept = pl.BlockSpec(memory_space=pltpu.VMEM)
    halo = jax.ShapeDtypeStruct((2 * lat, lev), jnp.float32)
    return pl.pallas_call(
        functools.partial(early_kernel, chunk, early),
        out_shape=[jax.ShapeDtypeStruct((early, width // 2, lev), jnp.bfloat16), halo, halo],
        in_specs=[anywhere] * 5,
        out_specs=[kept] * 3,
        scratch_shapes=[
            pltpu.VMEM((early, width, lev), jnp.float32),
            pltpu.VMEM((2, lat, PAD, lev), jnp.float32),
            pltpu.VMEM((2, 2 * lat, lev), jnp.float32),
            pltpu.VMEM((2, 2 * lat, lev), jnp.float32),
            pltpu.VMEM(w_in.shape, w_in.dtype),
            pltpu.VMEM(w_a.shape, w_a.dtype),
            pltpu.VMEM(w_b.shape, w_b.dtype),
            pltpu.VMEM(w_out.shape, w_out.dtype),
            pltpu.SemaphoreType.DMA((steps,)),
            pltpu.SemaphoreType.DMA((4,)),
            pltpu.SemaphoreType.DMA((2,)),
            pltpu.SemaphoreType.DMA((2,)),
            pltpu.SemaphoreType.DMA((2,)),
        ],
        compiler_params=pltpu.CompilerParams(
            vmem_limit_bytes=EARLY_MIB * 1024 * 1024, collective_id=0, has_side_effects=True
        ),
        cost_estimate=pl.CostEstimate(
            flops=early * width * 720896, bytes_accessed=4 * 1024 * 1024,
            transcendentals=early * width // 2 * 1536,
        ),
        name="early_part",
    )(x, w_in, w_a, w_b, w_out)


def column_kernel(chunk, early, x_hbm, lit_hbm, lon_hbm, lat_hbm, rates_hbm, low_hbm, high_hbm,
                  w_in_hbm, w_a_hbm, w_b_hbm, w_out_hbm,
                  out_hbm, xs, outs, coef, lit, early_rates, low, high, turned,
                  w_in, w_a, w_b, w_out, x_sems, w_sems, out_sems):
    lat, width, lev = x_hbm.shape
    cols = width // 2
    steps = lat // chunk
    ready = early // chunk

    def x_copy(i):
        return pltpu.make_async_copy(
            x_hbm.at[pl.ds(i * chunk, chunk)],
            xs.at[pl.ds(1 + i * chunk, chunk), pl.ds(PAD, width)],
            x_sems.at[i],
        )

    def out_copy(i):
        return pltpu.make_async_copy(
            outs.at[pl.ds(i * chunk, chunk)], out_hbm.at[pl.ds(i * chunk, chunk)], out_sems.at[i]
        )

    smalls = [
        pltpu.make_async_copy(source, target, w_sems.at[k])
        for k, (source, target) in enumerate([
            (low_hbm, low), (high_hbm, high), (lon_hbm, coef.at[pl.ds(0, lat)]),
            (lat_hbm, coef.at[pl.ds(lat, lat)]), (lit_hbm, lit),
            (w_in_hbm, w_in), (w_a_hbm, w_a), (w_b_hbm, w_b), (w_out_hbm, w_out),
            (rates_hbm, early_rates),
        ])
    ]
    x_copy(ready).start()
    for copy in smalls:
        copy.start()
    for i in (0, ready - 1):
        x_copy(i).start()
    for i in range(1, ready):
        x_copy(ready + i).start()
        if i < ready - 1:
            x_copy(i).start()

    blank = jnp.zeros((width, lev), jnp.float32)
    xs[0, pl.ds(PAD, width)] = blank
    xs[lat + 1, pl.ds(PAD, width)] = blank
    for copy in smalls:
        copy.wait()
    halved(w_in, w_a, w_b)
    half = 0.5 * coef[pl.ds(0, 2 * lat)]
    turned[...] = jnp.concatenate([
        half, lit[...].astype(jnp.float32), jnp.zeros((128 - 3 * lat, cols), jnp.float32)
    ], axis=0).T
    for r in range(lat):
        for f in range(2):
            xs[1 + r, pl.ds(PAD - 2 + f, 1)] = low[pl.ds(f * lat + r, 1)]
            xs[1 + r, pl.ds(PAD + width + f, 1)] = high[pl.ds(f * lat + r, 1)]
    for i in (ready, 0, ready - 1):
        x_copy(i).wait()

    def picked(r):
        at = jnp.full((cols, 128), r, jnp.int32)
        return jnp.take_along_axis(turned[...], at, axis=1, mode="promise_in_bounds")

    def move(first, rates):
        for q in range(chunk):
            r = first + q
            push_lon = picked(r)
            push_lat = picked(lat + r)
            lit_here = picked(2 * lat + r)
            heat = jnp.where(lit_here > 0.5, rates(q), 0.0)
            for f in range(2):
                mid = xs[1 + r, pl.ds(PAD + f, cols, stride=2), :]
                east = xs[1 + r, pl.ds(PAD + 2 + f, cols, stride=2), :]
                west = xs[1 + r, pl.ds(PAD - 2 + f, cols, stride=2), :]
                north = xs[2 + r, pl.ds(PAD + f, cols, stride=2), :]
                south = xs[r, pl.ds(PAD + f, cols, stride=2), :]
                new = (0.6 * mid + 0.1 * ((east + west) + (north + south))
                       - push_lon * (east - west) - push_lat * (north - south))
                if f == 0:
                    new = new + heat
                outs[r, pl.ds(f, cols, stride=2), :] = new

    def late_rates(first):
        rows = []
        for q in range(chunk):
            rows.append(jnp.concatenate([
                xs[1 + first + q, pl.ds(PAD + f, cols, stride=2), :].astype(jnp.bfloat16)
                for f in range(2)
            ], axis=1))
        return network(jnp.concatenate(rows, axis=0), (w_in, w_a, w_b), w_out)

    @pl.loop(0, ready)
    def _(i):
        @pl.when(i < ready - 1)
        def _():
            x_copy(i + 1 + ready).wait()

        @pl.when(i < ready - 2)
        def _():
            x_copy(i + 1).wait()

        late = (i + ready) * chunk
        rates = late_rates(late)
        soon = i * chunk
        move(soon, lambda q: early_rates[soon + q].astype(jnp.float32))
        out_copy(i).start()
        move(late, lambda q: rates[q * cols:(q + 1) * cols])
        out_copy(i + ready).start()

    @pl.loop(0, steps)
    def _(i):
        out_copy(i).wait()


def column_step(x, lit, lon, lat_push, rates, low, high, w_in, w_a, w_b, w_out, chunk, early):
    lat, width, lev = x.shape
    steps = lat // chunk
    anywhere = pl.BlockSpec(memory_space=pl.ANY)
    return pl.pallas_call(
        functools.partial(column_kernel, chunk, early),
        out_shape=jax.ShapeDtypeStruct(x.shape, jnp.float32),
        in_specs=[anywhere] * 11,
        out_specs=anywhere,
        scratch_shapes=[
            pltpu.VMEM((lat + 2, width + 2 * PAD, lev), jnp.float32),
            pltpu.VMEM(x.shape, jnp.float32),
            pltpu.VMEM((2 * lat, width // 2), jnp.float32),
            pltpu.VMEM(lit.shape, lit.dtype),
            pltpu.VMEM(rates.shape, rates.dtype),
            pltpu.VMEM(low.shape, low.dtype),
            pltpu.VMEM(high.shape, high.dtype),
            pltpu.VMEM((width // 2, 128), jnp.float32),
            pltpu.VMEM(w_in.shape, w_in.dtype),
            pltpu.VMEM(w_a.shape, w_a.dtype),
            pltpu.VMEM(w_b.shape, w_b.dtype),
            pltpu.VMEM(w_out.shape, w_out.dtype),
            pltpu.SemaphoreType.DMA((steps,)),
            pltpu.SemaphoreType.DMA((10,)),
            pltpu.SemaphoreType.DMA((steps,)),
        ],
        compiler_params=pltpu.CompilerParams(vmem_limit_bytes=56 * 1024 * 1024),
        cost_estimate=pl.CostEstimate(
            flops=(lat - early) * width * 720896, bytes_accessed=10 * 1024 * 1024,
            transcendentals=(lat - early) * width // 2 * 1536,
        ),
        name="column_step",
    )(x, lit, lon, lat_push, rates, low, high, w_in, w_a, w_b, w_out)


def shards(column_state, daylit, courant_lon, courant_lat, w_in, w_mid_a, w_mid_b, w_out):
    _, lat, cols, fields, lev = column_state.shape
    x = column_state.reshape(lat, cols * fields, lev)
    weights = (w_in, w_mid_a, w_mid_b, w_out)
    chunk, early = 4, lat // 2
    rates, low, high = early_part(x, *weights, chunk, early)
    out = column_step(
        x, daylit[0], courant_lon[0], courant_lat[0], rates, low, high, *weights, chunk, early
    )
    return out.reshape(column_state.shape)


def solution(mesh):
    placed = (
        P("groups", None, "lon", None, None),
        P("groups", None, "lon"),
        P("groups", None, "lon"),
        P("groups", None, "lon"),
        P(),
        P(),
        P(),
        P(),
    )
    return jax.shard_map(
        shards,
        mesh=mesh,
        in_specs=placed,
        out_specs=P("groups", None, "lon", None, None),
        check_vma=False,
    )
```

time: 27.8 us -> 20.6 us (0.74)
  Pallas kernels: 11.5 us -> 20.5 us
  waiting for transfers between devices: 5.66 us -> 0 us
  starting transfers between devices: 5.51 us -> 0 us
  local copies, waits for them, and re-layouts: 4.86 us -> 0 us
    pallas_call x1 -> x2, Pallas kernels: 11.5 us -> 20.5 us  [the longest x1 11 us: early_part(): pl.pallas_call(functools.partial(early_kernel, chunk, early), out_shape=[...]
    ppermute x2 -> x0, waiting for transfers between devices: 5.66 us -> none  [the longest x1 4.42 us: shards(): low = lax.ppermute(state[:, cols - 1].astype(jnp.bfloat16), 'lon', up)]
    ppermute x2 -> x0, starting transfers between devices: 5.51 us -> none  [the longest x1 5.51 us: shards(): high = lax.ppermute(state[:, 0].astype(jnp.bfloat16), 'lon', down)]
    unnamed x17 -> x0, local copies, waits for them, and re-layouts: 4.75 us -> none
  transfers between devices with their start and end apart: 2 -> 0, of which waited for: 2 -> 0; matrix products, arithmetic and copies ran while one was open for 1% -> 0% of each run, Pallas kernels for 0% -> 0%
where the time goes in v2:
time: 20.6 us; the launch traced here: 20.5 us
  Pallas kernels  20.5 us (100%)
    pallas_call x1, Pallas kernels, early_part(): pl.pallas_call(functools.partial(early_kernel, chunk, early), out_shape=[...  11 us
    pallas_call x1, Pallas kernels, column_step(): pl.pallas_call(functools.partial(column_kernel, chunk, early), out_shape=...  9.43 us

profile of v2, /device:TPU:0, one launch (start us, length us, event | category | flops | bytes accessed | tf_op | source)
XLA Modules:
  0.0 20.5 jit_solution(18234512002353711288)
XLA Ops:
  0.0 11.0 %early_part.1 = (bf16[16,128,128]{2,1,0:T(8,128)(2,1)}, f32[64,128]{1,0:T(8,128)}, f32[64,128]{1,0:T(8,128)}) custom-call(f32[32,256,128]{2,1,0:T(8,128)} %bitcast.5, bf16[256,512]{1,0:T(8,128)(2,1)} %w_in_hbm.3, bf16[512,512]{1,0:T(8,128)(2,1)} %w_a_hbm.3, bf16[512,512]{1,0:T(8,128)(2,1)} %w_b_hbm.3, bf16[512,128]{1,0:T(8,128)(2,1)} %w_out_hbm.3), custom_call_target="tpu_custom_call" | custom-call | flops 2952790016 | bytes 4194304 | tf_op jit(solution)/shard_map/early_part/pallas_call | solution.py:122
  11.1 9.4 %column_step.1 = f32[32,256,128]{2,1,0:T(8,128)} custom-call(f32[32,256,128]{2,1,0:T(8,128)} %bitcast.6, s32[32,128]{1,0:T(8,128)} %bitcast.7, f32[32,128]{1,0:T(8,128)} %bitcast.8, f32[32,128]{1,0:T(8,128)} %bitcast.9, bf16[16,128,128]{2,1,0:T(8,128)(2,1)} %get-tuple-element.8.rates_hbm, f32[64,128]{1,0:T(8,128)} %get-tuple-element.9.low_hbm, ...), custom_call_target="tpu_custom_call" | custom-call | flops 2952790016 | bytes 10485760 | tf_op jit(solution)/shard_map/column_step/pallas_call | solution.py:269

commit v3 on v1

v3 whole, which is shorter than its diff:
```python
import functools

import jax
import jax.numpy as jnp
from jax import lax
from jax.experimental import pallas as pl
from jax.experimental.pallas import tpu as pltpu
from jax.sharding import PartitionSpec as P

PAD = 8
KERNEL_MIB = 46


def silu_half(half):
    return half + half * jnp.tanh(half)


def halved(*weights):
    for w in weights:
        w[...] = w[...] * jnp.bfloat16(0.5)


def network(hidden, weights, w_out):
    for w in weights:
        hidden = silu_half(
            jnp.dot(hidden, w[...], preferred_element_type=jnp.float32)
        ).astype(jnp.bfloat16)
    return jnp.dot(hidden, w_out[...], preferred_element_type=jnp.float32)


def column_kernel(chunk, x_hbm, lit_hbm, lon_hbm, lat_hbm, w_in_hbm, w_a_hbm, w_b_hbm, w_out_hbm,
                  outs, xs, edges, packed, landed, coef, lit, turned, w_in, w_a, w_b, w_out,
                  x_sems, w_sems, edge_sems, send_sems, recv_sems):
    lat, width, lev = x_hbm.shape
    cols = width // 2
    steps = lat // chunk
    count = lax.axis_size("lon")
    me = lax.axis_index("lon")
    right = lax.rem(me + 1, count)
    left = lax.rem(me + count - 1, count)
    barrier = pltpu.get_barrier_semaphore()
    for other in (left, right):
        pl.semaphore_signal(
            barrier, inc=1, device_id={"lon": other}, device_id_type=pl.DeviceIdType.MESH
        )

    def x_copy(i):
        return pltpu.make_async_copy(
            x_hbm.at[pl.ds(i * chunk, chunk)],
            xs.at[pl.ds(1 + i * chunk, chunk), pl.ds(PAD, width)],
            x_sems.at[i],
        )

    edge_copies = [
        pltpu.make_async_copy(
            x_hbm.at[:, pl.ds(start, PAD)], edges.at[side], edge_sems.at[side]
        )
        for side, start in enumerate((0, width - PAD))
    ]
    smalls = [
        pltpu.make_async_copy(source, target, w_sems.at[k])
        for k, (source, target) in enumerate([
            (w_in_hbm, w_in), (lon_hbm, coef.at[pl.ds(0, lat)]),
            (lat_hbm, coef.at[pl.ds(lat, lat)]), (lit_hbm, lit),
            (w_a_hbm, w_a), (w_b_hbm, w_b), (w_out_hbm, w_out),
        ])
    ]
    for copy in edge_copies:
        copy.start()
    x_copy(0).start()
    for copy in smalls:
        copy.start()
    for i in range(1, steps):
        x_copy(i).start()

    sends = [
        pltpu.make_async_remote_copy(
            src_ref=packed.at[side], dst_ref=landed.at[side],
            send_sem=send_sems.at[side], recv_sem=recv_sems.at[side],
            device_id={"lon": other}, device_id_type=pl.DeviceIdType.MESH,
        )
        for side, other in enumerate((left, right))
    ]
    blank = jnp.zeros((width, lev), jnp.float32)
    xs[0, pl.ds(PAD, width)] = blank
    xs[lat + 1, pl.ds(PAD, width)] = blank
    nothing = jnp.zeros((lat, PAD, lev), jnp.float32)
    xs[pl.ds(1, lat), pl.ds(0, PAD)] = nothing
    xs[pl.ds(1, lat), pl.ds(PAD + width, PAD)] = nothing
    for side, copy in enumerate(edge_copies):
        copy.wait()
        for f in range(2):
            inner = f if side == 0 else PAD - 2 + f
            packed[side, pl.ds(f * lat, lat)] = edges[side, :, inner, :]
    for copy in smalls:
        copy.wait()
    halved(w_in, w_a, w_b)
    half = 0.5 * coef[...]
    turned[...] = jnp.concatenate([
        half, lit[...].astype(jnp.float32), jnp.zeros((128 - 3 * lat, cols), jnp.float32)
    ], axis=0).T
    x_copy(0).wait()

    def picked(r):
        at = jnp.full((cols, 128), r, jnp.int32)
        return jnp.take_along_axis(turned[...], at, axis=1, mode="promise_in_bounds")

    @pl.loop(0, steps)
    def _(i):
        @pl.when(i == 1)
        def _():
            pl.semaphore_wait(barrier, 2)
            for send in sends:
                send.start()

        @pl.when(i < steps - 1)
        def _():
            x_copy(i + 1).wait()

        first = i * chunk
        rows = [
            jnp.concatenate([
                xs[1 + first + q, pl.ds(PAD + f, cols, stride=2), :].astype(jnp.bfloat16)
                for f in range(2)
            ], axis=1)
            for q in range(chunk)
        ]
        rates = network(jnp.concatenate(rows, axis=0), (w_in, w_a, w_b), w_out)
        for q in range(chunk):
            r = first + q
            push_lon = picked(r)
            push_lat = picked(lat + r)
            lit_here = picked(2 * lat + r)
            heat = jnp.where(lit_here > 0.5, rates[q * cols:(q + 1) * cols], 0.0)
            for f in range(2):
                mid = xs[1 + r, pl.ds(PAD + f, cols, stride=2), :]
                east = xs[1 + r, pl.ds(PAD + 2 + f, cols, stride=2), :]
                west = xs[1 + r, pl.ds(PAD - 2 + f, cols, stride=2), :]
                north = xs[2 + r, pl.ds(PAD + f, cols, stride=2), :]
                south = xs[r, pl.ds(PAD + f, cols, stride=2), :]
                new = (0.6 * mid + 0.1 * ((east + west) + (north + south))
                       - push_lon * (east - west) - push_lat * (north - south))
                if f == 0:
                    new = new + heat
                outs[r, pl.ds(f, cols, stride=2), :] = new

    for send in sends:
        send.wait()
    from_west = 0.1 + 0.5 * coef[pl.ds(0, lat), 0:1]
    from_east = 0.1 - 0.5 * coef[pl.ds(0, lat), cols - 1:cols]
    for f in range(2):
        field = pl.ds(f * lat, lat)
        outs[:, f, :] = outs[:, f, :] + from_west * landed[1, field]
        outs[:, width - 2 + f, :] = outs[:, width - 2 + f, :] + from_east * landed[0, field]


def column_step(x, lit, lon, lat_push, w_in, w_a, w_b, w_out, chunk):
    lat, width, lev = x.shape
    steps = lat // chunk
    anywhere = pl.BlockSpec(memory_space=pl.ANY)
    return pl.pallas_call(
        functools.partial(column_kernel, chunk),
        out_shape=jax.ShapeDtypeStruct(x.shape, jnp.float32),
        in_specs=[anywhere] * 8,
        out_specs=pl.BlockSpec(memory_space=pltpu.VMEM),
        scratch_shapes=[
            pltpu.VMEM((lat + 2, width + 2 * PAD, lev), jnp.float32),
            pltpu.VMEM((2, lat, PAD, lev), jnp.float32),
            pltpu.VMEM((2, 2 * lat, lev), jnp.float32),
            pltpu.VMEM((2, 2 * lat, lev), jnp.float32),
            pltpu.VMEM((2 * lat, width // 2), jnp.float32),
            pltpu.VMEM(lit.shape, lit.dtype),
            pltpu.VMEM((width // 2, 128), jnp.float32),
            pltpu.VMEM(w_in.shape, w_in.dtype),
            pltpu.VMEM(w_a.shape, w_a.dtype),
            pltpu.VMEM(w_b.shape, w_b.dtype),
            pltpu.VMEM(w_out.shape, w_out.dtype),
            pltpu.SemaphoreType.DMA((steps,)),
            pltpu.SemaphoreType.DMA((7,)),
            pltpu.SemaphoreType.DMA((2,)),
            pltpu.SemaphoreType.DMA((2,)),
            pltpu.SemaphoreType.DMA((2,)),
        ],
        compiler_params=pltpu.CompilerParams(
            vmem_limit_bytes=KERNEL_MIB * 1024 * 1024, collective_id=0, has_side_effects=True
        ),
        cost_estimate=pl.CostEstimate(
            flops=lat * width * 720896, bytes_accessed=10 * 1024 * 1024,
            transcendentals=lat * width // 2 * 1536,
        ),
        name="column_step",
    )(x, lit, lon, lat_push, w_in, w_a, w_b, w_out)


def shards(column_state, daylit, courant_lon, courant_lat, w_in, w_mid_a, w_mid_b, w_out):
    _, lat, cols, fields, lev = column_state.shape
    out = column_step(
        column_state.reshape(lat, cols * fields, lev), daylit[0], courant_lon[0], courant_lat[0],
        w_in, w_mid_a, w_mid_b, w_out, 4
    )
    return out.reshape(column_state.shape)


def solution(mesh):
    placed = (
        P("groups", None, "lon", None, None),
        P("groups", None, "lon"),
        P("groups", None, "lon"),
        P("groups", None, "lon"),
        P(),
        P(),
        P(),
        P(),
    )
    return jax.shard_map(
        shards,
        mesh=mesh,
        in_specs=placed,
        out_specs=P("groups", None, "lon", None, None),
        check_vma=False,
    )
```

time: 27.8 us -> 22.4 us (0.81); the launches traced: 27.7 us -> 22 us
  waiting for transfers between devices: 5.66 us -> 0 us
  starting transfers between devices: 5.51 us -> 0 us
  local copies, waits for them, and re-layouts: 4.86 us -> 8.1 us
  Pallas kernels: 11.5 us -> 13.9 us
    ppermute x2 -> x0, waiting for transfers between devices: 5.66 us -> none  [the longest x1 4.42 us: shards(): low = lax.ppermute(state[:, cols - 1].astype(jnp.bfloat16), 'lon', up)]
    ppermute x2 -> x0, starting transfers between devices: 5.51 us -> none  [the longest x1 5.51 us: shards(): high = lax.ppermute(state[:, 0].astype(jnp.bfloat16), 'lon', down)]
    unnamed x17 -> x15, local copies, waits for them, and re-layouts: 4.75 us -> 8.1 us
    pallas_call x1, Pallas kernels: 11.5 us -> 13.9 us  [column_step(): pl.pallas_call(functools.partial(column_kernel, chunk), out_shape=jax.Sha...]
  transfers between devices with their start and end apart: 2 -> 0, of which waited for: 2 -> 0; matrix products, arithmetic and copies ran while one was open for 1% -> 0% of each run, Pallas kernels for 0% -> 0%
where the time goes in v3:
time: 22.4 us; the launch traced here: 22 us
  Pallas kernels  13.9 us (62%)
  local copies, waits for them, and re-layouts  8.1 us (36%)
    pallas_call x1, Pallas kernels, column_step(): pl.pallas_call(functools.partial(column_kernel, chunk), out_shape=jax.Sha...  13.9 us
    unnamed x15, local copies, waits for them, and re-layouts  8.1 us

profile of v3, /device:TPU:0, one launch (start us, length us, event | category | flops | bytes accessed | tf_op | source)
XLA Modules:
  0.0 22.0 jit_solution(2941681410124193695)
XLA Ops:
  0.0 0.0 copy-start
  0.0 1.0 %copy-done = bf16[512,512]{1,0:T(8,128)(2,1)S(1)} copy-done((bf16[512,512]{1,0:T(8,128)(2,1)S(1)}, bf16[512,512]{1,0:T(8,128)(2,1)}, u32[]{:S(2)}) %copy-start) | copy-done | bytes 524312
  1.0 0.0 copy-start.1
  1.0 1.0 %copy-done.1 = bf16[512,512]{1,0:T(8,128)(2,1)S(1)} copy-done((bf16[512,512]{1,0:T(8,128)(2,1)S(1)}, bf16[512,512]{1,0:T(8,128)(2,1)}, u32[]{:S(2)}) %copy-start.1) | copy-done | bytes 524312
  2.1 0.0 copy-start.2
  2.1 0.9 %copy-done.2 = bf16[256,512]{1,0:T(8,128)(2,1)S(1)} copy-done((bf16[256,512]{1,0:T(8,128)(2,1)S(1)}, bf16[256,512]{1,0:T(8,128)(2,1)}, u32[]{:S(2)}) %copy-start.2) | copy-done | bytes 262168
  3.0 0.0 copy-start.3
  3.0 0.9 %copy-done.3 = bf16[512,128]{1,0:T(8,128)(2,1)S(1)} copy-done((bf16[512,128]{1,0:T(8,128)(2,1)S(1)}, bf16[512,128]{1,0:T(8,128)(2,1)}, u32[]{:S(2)}) %copy-start.3) | copy-done | bytes 131096
  3.9 0.0 copy-start.4
  3.9 0.7 %copy-done.4 = s32[1,32,128]{2,1,0:T(8,128)S(1)} copy-done((s32[1,32,128]{2,1,0:T(8,128)S(1)}, s32[1,32,128]{2,1,0:T(8,128)}, u32[]{:S(2)}) %copy-start.4) | copy-done | bytes 16408
  4.7 0.0 copy-start.5
  4.7 0.7 %copy-done.5 = f32[1,32,128]{2,1,0:T(8,128)S(1)} copy-done((f32[1,32,128]{2,1,0:T(8,128)S(1)}, f32[1,32,128]{2,1,0:T(8,128)}, u32[]{:S(2)}) %copy-start.5) | copy-done | bytes 16408
  5.4 0.0 copy-start.6
  5.4 0.7 %copy-done.6 = f32[1,32,128]{2,1,0:T(8,128)S(1)} copy-done((f32[1,32,128]{2,1,0:T(8,128)S(1)}, f32[1,32,128]{2,1,0:T(8,128)}, u32[]{:S(2)}) %copy-start.6) | copy-done | bytes 16408
  6.1 13.9 %column_step.1 = f32[32,256,128]{2,1,0:T(8,128)S(1)} custom-call(f32[32,256,128]{2,1,0:T(8,128)} %bitcast.9, s32[32,128]{1,0:T(8,128)S(1)} %bitcast.6, f32[32,128]{1,0:T(8,128)S(1)} %bitcast.7, f32[32,128]{1,0:T(8,128)S(1)} %bitcast.8, bf16[256,512]{1,0:T(8,128)(2,1)S(1)} %copy-done.2, bf16[512,512]{1,0:T(8,128)(2,1)S(1)} %copy-done, ...), custom_call_target="tpu_custom_call" | custom-call | flops 5905580032 | bytes 10485760 | tf_op jit(solution)/shard_map/column_step/pallas_call | solution.py:161
  20.0 2.0 %copy.10 = f32[1,32,128,2,128]{4,3,2,1,0:T(2,128)} copy(f32[1,32,128,2,128]{4,3,2,1,0:T(2,128)S(1)} %bitcast.5) | data formatting | bytes 8388608
Async XLA Ops:
  0.0 1.0 %copy-start = (bf16[512,512]{1,0:T(8,128)(2,1)S(1)}, bf16[512,512]{1,0:T(8,128)(2,1)}, u32[]{:S(2)}) copy-start(bf16[512,512]{1,0:T(8,128)(2,1)} %w_a_hbm.1) | copy-start | bytes 1572868
  1.0 1.0 %copy-start.1 = (bf16[512,512]{1,0:T(8,128)(2,1)S(1)}, bf16[512,512]{1,0:T(8,128)(2,1)}, u32[]{:S(2)}) copy-start(bf16[512,512]{1,0:T(8,128)(2,1)} %w_b_hbm.1) | copy-start | bytes 1572868
  2.1 0.9 %copy-start.2 = (bf16[256,512]{1,0:T(8,128)(2,1)S(1)}, bf16[256,512]{1,0:T(8,128)(2,1)}, u32[]{:S(2)}) copy-start(bf16[256,512]{1,0:T(8,128)(2,1)} %w_in_hbm.1) | copy-start | bytes 786436
  3.0 0.9 %copy-start.3 = (bf16[512,128]{1,0:T(8,128)(2,1)S(1)}, bf16[512,128]{1,0:T(8,128)(2,1)}, u32[]{:S(2)}) copy-start(bf16[512,128]{1,0:T(8,128)(2,1)} %w_out_hbm.1) | copy-start | bytes 393220
  3.9 0.7 %copy-start.4 = (s32[1,32,128]{2,1,0:T(8,128)S(1)}, s32[1,32,128]{2,1,0:T(8,128)}, u32[]{:S(2)}) copy-start(s32[1,32,128]{2,1,0:T(8,128)} %param.9) | copy-start | bytes 49156
  4.7 0.7 %copy-start.5 = (f32[1,32,128]{2,1,0:T(8,128)S(1)}, f32[1,32,128]{2,1,0:T(8,128)}, u32[]{:S(2)}) copy-start(f32[1,32,128]{2,1,0:T(8,128)} %param.10) | copy-start | bytes 49156
  5.4 0.7 %copy-start.6 = (f32[1,32,128]{2,1,0:T(8,128)S(1)}, f32[1,32,128]{2,1,0:T(8,128)}, u32[]{:S(2)}) copy-start(f32[1,32,128]{2,1,0:T(8,128)} %param.11) | copy-start | bytes 49156

commit v4 on v3

--- a/solution.py
+++ b/solution.py
@@ -157,7 +157,7 @@
 def column_step(x, lit, lon, lat_push, w_in, w_a, w_b, w_out, chunk):
     lat, width, lev = x.shape
     steps = lat // chunk
-    anywhere = pl.BlockSpec(memory_space=pl.ANY)
+    anywhere = pl.BlockSpec(memory_space=pltpu.HBM)
     return pl.pallas_call(
         functools.partial(column_kernel, chunk),
         out_shape=jax.ShapeDtypeStruct(x.shape, jnp.float32),

time: 22.4 us -> 22.4 us (level)
  no operation moved by 1% of the time
where the time goes in v4:
time: 22.4 us; the launch traced here: 22 us
  Pallas kernels  13.9 us (62%)
  local copies, waits for them, and re-layouts  8.1 us (36%)
    pallas_call x1, Pallas kernels, column_step(): pl.pallas_call(functools.partial(column_kernel, chunk), out_shape=jax.Sha...  13.9 us
    unnamed x15, local copies, waits for them, and re-layouts  8.1 us

profile of v4, /device:TPU:0, one launch (start us, length us, event | category | flops | bytes accessed | tf_op | source)
XLA Modules:
  0.0 22.0 jit_solution(2941681410124193695)
XLA Ops:
  0.0 0.0 copy-start
  0.0 1.0 %copy-done = bf16[512,512]{1,0:T(8,128)(2,1)S(1)} copy-done((bf16[512,512]{1,0:T(8,128)(2,1)S(1)}, bf16[512,512]{1,0:T(8,128)(2,1)}, u32[]{:S(2)}) %copy-start) | copy-done | bytes 524312
  1.0 0.0 copy-start.1
  1.0 1.0 %copy-done.1 = bf16[512,512]{1,0:T(8,128)(2,1)S(1)} copy-done((bf16[512,512]{1,0:T(8,128)(2,1)S(1)}, bf16[512,512]{1,0:T(8,128)(2,1)}, u32[]{:S(2)}) %copy-start.1) | copy-done | bytes 524312
  2.1 0.0 copy-start.2
  2.1 0.9 %copy-done.2 = bf16[256,512]{1,0:T(8,128)(2,1)S(1)} copy-done((bf16[256,512]{1,0:T(8,128)(2,1)S(1)}, bf16[256,512]{1,0:T(8,128)(2,1)}, u32[]{:S(2)}) %copy-start.2) | copy-done | bytes 262168
  3.0 0.0 copy-start.3
  3.0 0.9 %copy-done.3 = bf16[512,128]{1,0:T(8,128)(2,1)S(1)} copy-done((bf16[512,128]{1,0:T(8,128)(2,1)S(1)}, bf16[512,128]{1,0:T(8,128)(2,1)}, u32[]{:S(2)}) %copy-start.3) | copy-done | bytes 131096
  3.9 0.0 copy-start.4
  3.9 0.7 %copy-done.4 = s32[1,32,128]{2,1,0:T(8,128)S(1)} copy-done((s32[1,32,128]{2,1,0:T(8,128)S(1)}, s32[1,32,128]{2,1,0:T(8,128)}, u32[]{:S(2)}) %copy-start.4) | copy-done | bytes 16408
  4.7 0.0 copy-start.5
  4.7 0.7 %copy-done.5 = f32[1,32,128]{2,1,0:T(8,128)S(1)} copy-done((f32[1,32,128]{2,1,0:T(8,128)S(1)}, f32[1,32,128]{2,1,0:T(8,128)}, u32[]{:S(2)}) %copy-start.5) | copy-done | bytes 16408
  5.4 0.0 copy-start.6
  5.4 0.7 %copy-done.6 = f32[1,32,128]{2,1,0:T(8,128)S(1)} copy-done((f32[1,32,128]{2,1,0:T(8,128)S(1)}, f32[1,32,128]{2,1,0:T(8,128)}, u32[]{:S(2)}) %copy-start.6) | copy-done | bytes 16408
  6.1 13.9 %column_step.1 = f32[32,256,128]{2,1,0:T(8,128)S(1)} custom-call(f32[32,256,128]{2,1,0:T(8,128)} %bitcast.9, s32[32,128]{1,0:T(8,128)S(1)} %bitcast.6, f32[32,128]{1,0:T(8,128)S(1)} %bitcast.7, f32[32,128]{1,0:T(8,128)S(1)} %bitcast.8, bf16[256,512]{1,0:T(8,128)(2,1)S(1)} %copy-done.2, bf16[512,512]{1,0:T(8,128)(2,1)S(1)} %copy-done, ...), custom_call_target="tpu_custom_call" | custom-call | flops 5905580032 | bytes 10485760 | tf_op jit(solution)/shard_map/column_step/pallas_call | solution.py:161
  20.0 2.0 %copy.10 = f32[1,32,128,2,128]{4,3,2,1,0:T(2,128)} copy(f32[1,32,128,2,128]{4,3,2,1,0:T(2,128)S(1)} %bitcast.5) | data formatting | bytes 8388608
Async XLA Ops:
  0.0 1.0 %copy-start = (bf16[512,512]{1,0:T(8,128)(2,1)S(1)}, bf16[512,512]{1,0:T(8,128)(2,1)}, u32[]{:S(2)}) copy-start(bf16[512,512]{1,0:T(8,128)(2,1)} %w_a_hbm.1) | copy-start | bytes 1572868
  1.0 1.0 %copy-start.1 = (bf16[512,512]{1,0:T(8,128)(2,1)S(1)}, bf16[512,512]{1,0:T(8,128)(2,1)}, u32[]{:S(2)}) copy-start(bf16[512,512]{1,0:T(8,128)(2,1)} %w_b_hbm.1) | copy-start | bytes 1572868
  2.1 0.9 %copy-start.2 = (bf16[256,512]{1,0:T(8,128)(2,1)S(1)}, bf16[256,512]{1,0:T(8,128)(2,1)}, u32[]{:S(2)}) copy-start(bf16[256,512]{1,0:T(8,128)(2,1)} %w_in_hbm.1) | copy-start | bytes 786436
  3.0 0.9 %copy-start.3 = (bf16[512,128]{1,0:T(8,128)(2,1)S(1)}, bf16[512,128]{1,0:T(8,128)(2,1)}, u32[]{:S(2)}) copy-start(bf16[512,128]{1,0:T(8,128)(2,1)} %w_out_hbm.1) | copy-start | bytes 393220
  3.9 0.7 %copy-start.4 = (s32[1,32,128]{2,1,0:T(8,128)S(1)}, s32[1,32,128]{2,1,0:T(8,128)}, u32[]{:S(2)}) copy-start(s32[1,32,128]{2,1,0:T(8,128)} %param.9) | copy-start | bytes 49156
  4.7 0.7 %copy-start.5 = (f32[1,32,128]{2,1,0:T(8,128)S(1)}, f32[1,32,128]{2,1,0:T(8,128)}, u32[]{:S(2)}) copy-start(f32[1,32,128]{2,1,0:T(8,128)} %param.10) | copy-start | bytes 49156
  5.4 0.7 %copy-start.6 = (f32[1,32,128]{2,1,0:T(8,128)S(1)}, f32[1,32,128]{2,1,0:T(8,128)}, u32[]{:S(2)}) copy-start(f32[1,32,128]{2,1,0:T(8,128)} %param.11) | copy-start | bytes 49156
